TPU v7x, 32 devices: a whole 2x2x4 slice. The times are simulated.
32 devices in a mesh: frames: 32 (over z, y, x, core), centers: 1.
Axes of the slice: x: 2, y: 2, z: 4, core: 2. Of those that a mesh axis runs over, the one named last changes fastest.
Arguments:
- frames: bfloat16 [32768, 512], P('frames'), may hold values from -24 to 24
- centers: bfloat16 [16384, 512], P('centers'), may hold values from -6 to 6
- starts: int32 [64], replicated, may hold values from 0 to 32767, as said below
Outputs:
- counts: float32 [512, 16384], P('frames', 'centers')
Inputs may be any that keep to these rules, and one draw needn't show every extreme that they name: starts[0] is 0 and the entries rise strictly.
All inputs are finite; a program needn't handle non-finite values.
Results may differ from a plain program's by a relative error of at most 0.001.
Values may be sent and summed in bfloat16 or wider, within the bound.
A program may use at most 192 MiB of HBM per device.

v0:
```python
import jax
import jax.numpy as jnp
from jax import lax
from jax.sharding import PartitionSpec as P

K = 16384
W = 512
LAG = 5


SHARPNESS = 0.03125


def broadcast(shard, axis, root):
    mine = lax.axis_index(axis) == root
    return lax.psum(jnp.where(mine, shard, jnp.zeros_like(shard)), axis)


def passed_along(block, axis, distance):
    devices = range(lax.axis_size(axis))
    route = [(i - distance, i) for i in devices if i - distance in devices]
    return lax.ppermute(block, axis, route)


def logits_of(row_block, centers):
    inner_prod = lax.dot_general(
        row_block, centers, (((1,), (1,)), ((), ())), preferred_element_type=jnp.float32
    )
    frame_norm = jnp.sum(row_block.astype(jnp.float32) ** 2, axis=1, keepdims=True)
    center_norm = jnp.sum(centers.astype(jnp.float32) ** 2, axis=1)
    return -SHARPNESS * (frame_norm - 2.0 * inner_prod + center_norm[None, :])


def segment_of(positions, starts):
    return jnp.sum((starts[None, :] <= positions[:, None]).astype(jnp.int32), axis=1)


def shards(frames, centers, starts):
    frame_count = frames.shape[0]
    logits = logits_of(frames, centers)
    row_top = lax.pmax(jnp.max(logits, axis=1), "centers")
    exponent = jnp.exp(logits - row_top[:, None])
    row_total = lax.psum(jnp.sum(exponent, axis=1), "centers")
    member = (exponent / row_total[:, None]).astype(jnp.bfloat16)
    window_member = broadcast(member[:, :W], "centers", 0)
    following = passed_along(member[:LAG], "frames", -1)
    lag_rows = jnp.concatenate([member[LAG:], following], axis=0)
    total_frames = frame_count * lax.axis_size("frames")
    positions = lax.axis_index("frames") * frame_count + jnp.arange(frame_count, dtype=jnp.int32)
    later = positions + LAG
    usable = jnp.logical_and(
        segment_of(positions, starts) == segment_of(later, starts), later < total_frames
    )
    lead_rows = window_member * usable[:, None].astype(jnp.bfloat16)
    owners = lax.axis_size("frames")
    owned_rows = W // owners
    partial_value = lax.dot_general(
        lead_rows, lag_rows, (((0,), (0,)), ((), ())), preferred_element_type=jnp.float32
    )
    pieces = partial_value.reshape(owners, owned_rows, partial_value.shape[1])
    received = lax.all_to_all(
        pieces.astype(jnp.bfloat16), "frames", split_axis=0, concat_axis=0, tiled=True
    ).astype(pieces.dtype)
    summed = jnp.sum(received, axis=0)
    return summed * (K * K / total_frames)


def solution(mesh):
    return jax.shard_map(
        shards,
        mesh=mesh,
        in_specs=(P("frames", None), P("centers", None), P()),
        out_specs=P("frames", "centers"),
        check_vma=False,
    )
```

profile of v0, /device:TPU:0, one launch (start us, length us, event | category | flops | bytes accessed | tf_op | source)
XLA Modules:
  0.0 522.8 jit_solution(6558118536413176579)
XLA Ops:
  0.0 7.2 %multiply_reduce_fusion = f32[16384]{0:T(1024)S(1)} fusion(bf16[16384,512]{1,0:T(8,128)(2,1)} %param.4), kind=kLoop, calls=%fused_computation.10 | loop fusion | flops 25149440 | bytes 16842752 | tf_op jit(solution)/shard_map/reduce_sum | solution.py:30
  7.2 1.5 multiply_reduce_fusion.1
  8.7 31.9 %fusion.1 = (f32[1024]{0:T(1024)S(1)}, f32[1024,16384]{1,0:T(8,128)}) fusion(f32[16384]{0:T(1024)S(1)} %multiply_reduce_fusion, f32[1024]{0:T(1024)S(1)} %multiply_reduce_fusion.1, bf16[1024,512]{1,0:T(8,128)(2,1)} %param.3, bf16[16384,512]{1,0:T(8,128)(2,1)} %param.4), kind=kOutput, calls=%fused_computation.4 | convolution fusion | flops 17263755264 | bytes 85008384 | tf_op jit(solution)/shard_map/dot_general | solution.py:26
  40.6 22.0 %fusion = f32[1024]{0:T(1024)S(1)} fusion(f32[1024,16384]{1,0:T(8,128)} %get-tuple-element.8, f32[1024]{0:T(1024)S(1)} %get-tuple-element.7, f32[16384]{0:T(1024)S(1)} %multiply_reduce_fusion, f32[1024]{0:T(1024)S(1)} %multiply_reduce_fusion.1), kind=kLoop, calls=%fused_computation.3 | loop fusion | flops 100662272 | bytes 67186688 | tf_op jit(solution)/shard_map/reduce_sum | solution.py:43
  62.6 0.0 copy-start
  62.6 33.5 %divide_convert_fusion = bf16[1024,16384]{1,0:T(8,128)(2,1)} fusion(f32[1024,16384]{1,0:T(8,128)} %get-tuple-element.8, f32[1024]{0:T(1024)S(1)} %fusion, f32[1024]{0:T(1024)S(1)} %get-tuple-element.7, f32[16384]{0:T(1024)S(1)} %multiply_reduce_fusion, f32[1024]{0:T(1024)S(1)} %multiply_reduce_fusion.1), kind=kLoop, calls=%fused_computation | loop fusion | flops 117440512 | bytes 100741120 | tf_op jit(solution)/shard_map/convert_element_type | solution.py:44
  96.1 1.0 slice.14
  97.0 1.5 collective-permute-start
  98.5 23.3 %slice.13 = bf16[1019,16384]{1,0:T(8,128)(2,1)} slice(bf16[1024,16384]{1,0:T(8,128)(2,1)} %divide_convert_fusion), slice={[5:1024], [0:16384]} | slice | bytes 66781184 | tf_op jit(solution)/shard_map/slice | solution.py:47
  121.8 0.0 copy-done
  121.8 0.1 convert_reduce_fusion.1
  122.0 0.0 collective-permute-done
  122.0 26.0 %fusion.6 = bf16[512,16384]{1,0:T(8,128)(2,1)} fusion(bf16[5,16384]{1,0:T(8,128)(2,1)S(1)} %collective-permute-done, bf16[1019,16384]{1,0:T(8,128)(2,1)} %slice.13, bf16[1024,16384]{1,0:T(8,128)(2,1)} %divide_convert_fusion, bf16[1024]{0:T(1024)(128)(2,1)S(1)} %and_convert_fusion), kind=kOutput, calls=%fused_computation.11 | convolution fusion | flops 17255890944 | bytes 51546112 | tf_op jit(solution)/shard_map/dot_general | solution.py:57
  148.0 371.4 %all_to_all.5 = bf16[32,16,16384]{2,1,0:T(8,128)(2,1)S(1)} all-to-all(bf16[32,16,16384]{2,1,0:T(8,128)(2,1)} %bitcast.3), channel_id=1, replica_groups=mesh['frames'=32,'centers'=1] {'frames'}, dimensions={0} | all-to-all | bytes 33554432 | tf_op jit(solution)/shard_map/all_to_all | solution.py:61
  519.3 2.5 convert_reduce_fusion
  521.8 1.0 broadcast_multiply_fusion
  (2 shorter events, 0.0 us)
Async XLA Ops:
  62.6 59.2 %copy-start = (s32[64]{0:T(128)S(1)}, s32[64]{0:T(128)}, u32[]{:S(2)}) copy-start(s32[64]{0:T(128)} %param.5) | copy-start | bytes 772
  97.0 24.9 %collective-permute-start = (bf16[5,16384]{1,0:T(8,128)(2,1)S(1)}, bf16[5,16384]{1,0:T(8,128)(2,1)S(1)}, u32[]{:S(2)}, u32[]{:S(2)}) collective-permute-start(bf16[5,16384]{1,0:T(8,128)(2,1)S(1)} %slice.14), channel_id=1, source_target_pairs={{1,0},{2,1},{3,2},{4,3},{5,4},{6,5},{7,6},{8,7},{9,8},{10,9},{11,1... | collective-permute-start | bytes 491528 | tf_op jit(solution)/shard_map/ppermute | solution.py:22
where the time goes:
time: 523 us
  blocking collectives  371 us (71%)
  other arithmetic  67.8 us (13%)
  matrix products  57.8 us (11%)
  local copies, waits for them, and re-layouts  24.3 us (5%)
    all_to_all x1, blocking collectives, shards(): lax.all_to_all(pieces.astype(jnp.bfloat16), 'frames', split_axis=0, conca...  371 us
    convert_element_type x1, other arithmetic, shards(): member = (exponent / row_total[:, None]).astype(jnp.bfloat16)  33.5 us
    dot_general x1, matrix products, logits_of(): lax.dot_general(row_block, centers, (((1,), (1,)), ((), ())), preferred_e...  31.9 us
    dot_general x1, matrix products, shards(): lax.dot_general(lead_rows, lag_rows, (((0,), (0,)), ((), ())), preferred_...  26 us
    slice x1, local copies, waits for them, and re-layouts, shards(): lag_rows = jnp.concatenate([member[LAG:], following], axis=0)  23.3 us
    reduce_sum x1, other arithmetic, shards(): row_total = lax.psum(jnp.sum(exponent, axis=1), 'centers')  22 us
  transfers between devices with their start and end apart: 1, of which 0 were waited for; matrix products, arithmetic and copies ran while one was open for 4% of the time, Pallas kernels for 0%

commit v1 on v0

v1 whole, which is shorter than its diff:
```python
import math

import jax
import jax.numpy as jnp
from jax import lax
from jax.experimental import pallas as pl
from jax.experimental.pallas import tpu as pltpu
from jax.sharding import PartitionSpec as P

K = 16384
W = 512
LAG = 5
GROUP = 8
HALO = 128
TAIL = 16
TILE = 512
SHARPNESS = 0.03125
ALPHA = 2.0 * SHARPNESS * math.log2(math.e)
VMEM_BYTES = 56 * 1024 * 1024
TRANS_B = (((1,), (1,)), ((), ()))


def weights_of(points, norms, rows):
    score = (
        lax.dot_general(points, rows, TRANS_B, preferred_element_type=jnp.float32) - norms
    )
    top = jnp.max(score, axis=0, keepdims=True)
    return top, jnp.exp2(ALPHA * (score - top))


def member_kernel(
    rows_ref, halo_ref, centers_ref, center_norm_ref, source_ref, source_norm_ref,
    member_ref, lead_ref, top_ref, sum_ref, lead_top_ref,
    halo_top_ref, halo_sum_ref, halo_lead_top_ref, carry_ref,
):
    step = pl.program_id(0)

    @pl.when(step == 0)
    def _():
        rows = halo_ref[...]
        top, weight = weights_of(centers_ref[...], center_norm_ref[...], rows)
        halo_top_ref[...] = top
        halo_sum_ref[...] = jnp.sum(weight, axis=0, keepdims=True)
        top, weight = weights_of(source_ref[...], source_norm_ref[...], rows)
        halo_lead_top_ref[...] = top
        carry_ref[...] = pltpu.roll(weight, LAG, 1)

    @pl.when(step > 0)
    def _():
        rows = rows_ref[...]
        top, weight = weights_of(centers_ref[...], center_norm_ref[...], rows)
        top_ref[...] = top
        sum_ref[...] = jnp.sum(weight, axis=0, keepdims=True)
        member_ref[...] = weight.astype(jnp.bfloat16)
        top, weight = weights_of(source_ref[...], source_norm_ref[...], rows)
        lead_top_ref[...] = top
        moved = pltpu.roll(weight, LAG, 1)
        lane = lax.broadcasted_iota(jnp.int32, (W, HALO), 1)
        first = moved[:, :HALO]
        lead_ref[:, :HALO] = jnp.where(lane < LAG, carry_ref[...], first).astype(jnp.bfloat16)
        lead_ref[:, HALO:] = moved[:, HALO:].astype(jnp.bfloat16)
        carry_ref[...] = first


def members(rows, halo, centers, center_norm, source, source_norm):
    frame_count, depth = rows.shape
    states = centers.shape[0]
    steps = frame_count // TILE
    whole = lambda i: (0, 0)
    along = lambda i: (0, jnp.maximum(i - 1, 0))
    stat = jax.ShapeDtypeStruct((1, frame_count), jnp.float32)
    halo_stat = jax.ShapeDtypeStruct((1, HALO), jnp.float32)
    return pl.pallas_call(
        member_kernel,
        grid=(steps + 1,),
        in_specs=[
            pl.BlockSpec((TILE, depth), lambda i: (jnp.maximum(i - 1, 0), 0)),
            pl.BlockSpec((HALO, depth), whole),
            pl.BlockSpec((states, depth), whole),
            pl.BlockSpec((states, 1), whole),
            pl.BlockSpec((W, depth), whole),
            pl.BlockSpec((W, 1), whole),
        ],
        out_specs=[
            pl.BlockSpec((states, TILE), along),
            pl.BlockSpec((W, TILE), along),
            pl.BlockSpec((1, TILE), along),
            pl.BlockSpec((1, TILE), along),
            pl.BlockSpec((1, TILE), along),
            pl.BlockSpec((1, HALO), whole),
            pl.BlockSpec((1, HALO), whole),
            pl.BlockSpec((1, HALO), whole),
        ],
        out_shape=[
            jax.ShapeDtypeStruct((states, frame_count), jnp.bfloat16),
            jax.ShapeDtypeStruct((W, frame_count), jnp.bfloat16),
            stat, stat, stat, halo_stat, halo_stat, halo_stat,
        ],
        scratch_shapes=[pltpu.VMEM((W, HALO), jnp.float32)],
        compiler_params=pltpu.CompilerParams(vmem_limit_bytes=VMEM_BYTES),
        cost_estimate=pl.CostEstimate(
            flops=2 * frame_count * depth * (states + W),
            bytes_accessed=2 * frame_count * (states + W + depth),
            transcendentals=frame_count * (states + W),
        ),
        name="members",
    )(rows, halo, centers, center_norm, source, source_norm)


def counts_kernel(lead_ref, scale_ref, member_ref, out_ref):
    @pl.when(pl.program_id(0) == 0)
    def _():
        out_ref[...] = jnp.zeros_like(out_ref)

    lead = (lead_ref[...].astype(jnp.float32) * scale_ref[...]).astype(jnp.bfloat16)
    out_ref[...] += lax.dot_general(
        lead, member_ref[...], TRANS_B, preferred_element_type=jnp.float32
    )


def counts_of(lead, scale, member):
    states, frame_count = member.shape
    tile = 2 * TILE
    return pl.pallas_call(
        counts_kernel,
        grid=(frame_count // tile,),
        in_specs=[
            pl.BlockSpec((W, tile), lambda i: (0, i)),
            pl.BlockSpec((1, tile), lambda i: (0, i)),
            pl.BlockSpec((states, tile), lambda i: (0, i)),
        ],
        out_specs=pl.BlockSpec((W, states), lambda i: (0, 0)),
        out_shape=jax.ShapeDtypeStruct((W, states), jnp.float32),
        compiler_params=pltpu.CompilerParams(vmem_limit_bytes=VMEM_BYTES),
        cost_estimate=pl.CostEstimate(
            flops=2 * frame_count * W * states,
            bytes_accessed=2 * frame_count * (states + W),
            transcendentals=0,
        ),
        name="counts",
    )(lead, scale, member)


def segment_of(positions, starts):
    return jnp.sum((starts[:, None] <= positions[None, :]).astype(jnp.int32), axis=0)


def half_norm(points):
    return 0.5 * jnp.sum(points.astype(jnp.float32) ** 2, axis=1, keepdims=True)


def shards(frames, centers, starts):
    device_frames, depth = frames.shape
    devices = lax.axis_size("frames")
    planes = devices // GROUP
    me = lax.axis_index("frames")
    plane, place = me // GROUP, me % GROUP
    groups = [[p * GROUP + c for c in range(GROUP)] for p in range(planes)]

    tails = lax.all_gather(frames[-TAIL:], "frames")
    rows = lax.all_gather(frames, "frames", axis_index_groups=groups, tiled=True)
    before = lax.dynamic_index_in_dim(
        tails, jnp.maximum(plane * GROUP - 1, 0), 0, keepdims=False
    )
    halo = jnp.concatenate([jnp.zeros((HALO - TAIL, depth), frames.dtype), before], axis=0)

    states = centers.shape[0] // GROUP
    own = lax.dynamic_slice_in_dim(centers, place * states, states, 0)
    source = centers[:W]
    if lax.axis_size("centers") > 1:
        mine = lax.axis_index("centers") == 0
        source = lax.psum(jnp.where(mine, source, jnp.zeros_like(source)), "centers")

    member, lead, top, total, lead_top, halo_top, halo_total, halo_lead_top = members(
        rows, halo, own, half_norm(own), source, half_norm(source)
    )

    stats = jnp.concatenate(
        [
            jnp.concatenate([halo_top, top], axis=1),
            jnp.concatenate([halo_total, total], axis=1),
        ],
        axis=0,
    )
    gathered = lax.all_gather(stats, "frames", axis_index_groups=groups)
    all_top = lax.pmax(jnp.max(gathered[:, 0], axis=0), "centers")
    all_total = lax.psum(
        jnp.sum(gathered[:, 1] * jnp.exp2(ALPHA * (gathered[:, 0] - all_top)), axis=0),
        "centers",
    )

    plane_frames = rows.shape[0]
    positions = plane * plane_frames - HALO + jnp.arange(plane_frames + HALO, dtype=jnp.int32)
    usable = jnp.logical_and(
        segment_of(positions, starts) == segment_of(positions + LAG, starts),
        jnp.logical_and(positions >= 0, positions + LAG < plane_frames * planes),
    )
    lead_tops = jnp.concatenate([halo_lead_top, lead_top], axis=1)[0]
    lead_factor = jnp.where(usable, jnp.exp2(ALPHA * (lead_tops - all_top)) / all_total, 0.0)
    lag_factor = jnp.exp2(ALPHA * (top[0] - all_top[HALO:])) / all_total[HALO:]
    scale = lead_factor[HALO - LAG : HALO - LAG + plane_frames] * lag_factor

    partial = counts_of(lead, scale[None, :], member)

    row_top = jnp.max(partial, axis=1, keepdims=True)
    power = jnp.clip(jnp.floor(jnp.log2(jnp.maximum(row_top, 1e-30))), -100.0, 100.0)
    scaled = (partial * jnp.exp2(14.0 - power)).astype(jnp.float16)
    sent = jnp.concatenate(
        [scaled, jnp.broadcast_to(power.astype(jnp.float16), (W, 128))], axis=1
    )
    owned = W // devices
    received = lax.all_to_all(
        sent.reshape(devices, owned, states + 128), "frames", split_axis=0, concat_axis=0, tiled=True
    ).astype(jnp.float32)
    unit = jnp.exp2(received[:, :, states : states + 1] - 14.0)
    summed = jnp.sum(
        (received[:, :, :states] * unit).reshape(planes, GROUP, owned, states), axis=0
    )
    summed = summed * (K * K / (plane_frames * planes))
    return summed.transpose(1, 0, 2).reshape(owned, GROUP * states)


def solution(mesh):
    return jax.shard_map(
        shards,
        mesh=mesh,
        in_specs=(P("frames", None), P("centers", None), P()),
        out_specs=P("frames", "centers"),
        check_vma=False,
    )
```

time: 523 us -> 270 us (0.52)
  blocking collectives: 371 us -> 112 us
  Pallas kernels: 0 us -> 75.4 us
  matrix products: 57.8 us -> 0 us
  other arithmetic: 67.8 us -> 28.2 us
  between operations: 0.08 us -> 13.5 us
  local copies, waits for them, and re-layouts: 24.3 us -> 32.4 us
  waiting for transfers between devices: 0.01 us -> 7.3 us
    all_to_all x1, blocking collectives: 371 us -> 57.2 us  [shards(): lax.all_to_all(sent.reshape(devices, owned, states + 128), 'frames', spli...]
    pallas_call x0 -> x2, Pallas kernels: none -> 75.4 us  [the longest x1 51.2 us: members(): pl.pallas_call(member_kernel, grid=(steps + 1,), in_specs=[pl.BlockSpec((...]
    dot_general x2 -> x0, matrix products: 57.8 us -> none  [the longest x1 31.9 us: logits_of(): lax.dot_general(row_block, centers, (((1,), (1,)), ((), ())), preferred_e...]
    all_gather x0 -> x2, blocking collectives: none -> 55.2 us  [the longest x1 45.3 us: shards(): tails = lax.all_gather(frames[-TAIL:], 'frames')]
    convert_element_type x2, other arithmetic: 33.5 us -> 7.4 us  [the longest x1 4.8 us: shards(): received = lax.all_to_all(sent.reshape(devices, owned, states + 128), 'fr...]
    reduce_sum x5, other arithmetic: 33.3 us -> 7.85 us  [the longest x2 4.51 us: half_norm(): return 0.5 * jnp.sum(points.astype(jnp.float32) ** 2, axis=1, keepdims=True)]
    slice x2, local copies, waits for them, and re-layouts: 24.3 us -> 2.61 us  [the longest x1 1.89 us: shards(): source = centers[:W]]
    mul x0 -> x3, local copies, waits for them, and re-layouts: none -> 14.2 us  [the longest x1 12 us: shards(): received[:, :, :states] * unit]
  transfers between devices with their start and end apart: 1 -> 1, of which waited for: 0 -> 1; matrix products, arithmetic and copies ran while one was open for 4% -> 4% of each run, Pallas kernels for 0% -> 0%
where the time goes in v1:
time: 270 us; the launch traced here: 269 us
  blocking collectives  112 us (41%)
  Pallas kernels  75.4 us (28%)
  local copies, waits for them, and re-layouts  32.4 us (12%)
  other arithmetic  28.2 us (10%)
  between operations  13.5 us (5%)
  waiting for transfers between devices  7.3 us (3%)
    all_to_all x1, blocking collectives, shards(): lax.all_to_all(sent.reshape(devices, owned, states + 128), 'frames', spli...  57.2 us
    pallas_call x1, Pallas kernels, members(): pl.pallas_call(member_kernel, grid=(steps + 1,), in_specs=[pl.BlockSpec((...  51.2 us
    all_gather x1, blocking collectives, shards(): tails = lax.all_gather(frames[-TAIL:], 'frames')  45.3 us
    pallas_call x1, Pallas kernels, counts_of(): pl.pallas_call(counts_kernel, grid=(frame_count // tile,), in_specs=[pl.B...  24.3 us
    all_to_all x1, local copies, waits for them, and re-layouts, shards(): lax.all_to_all(sent.reshape(devices, owned, states + 128), 'frames', spli...  13.7 us
    mul x1, local copies, waits for them, and re-layouts, shards(): received[:, :, :states] * unit  12 us
    all_gather x1, blocking collectives, shards(): gathered = lax.all_gather(stats, 'frames', axis_index_groups=groups)  9.86 us
    all_gather x1, waiting for transfers between devices, shards(): lax.all_gather(frames, 'frames', axis_index_groups=groups, tiled=True)  6.59 us
  transfers between devices with their start and end apart: 1, of which 1 were waited for; matrix products, arithmetic and copies ran while one was open for 4% of the time, Pallas kernels for 0%

profile of v1, /device:TPU:0, one launch (start us, length us, event | category | flops | bytes accessed | tf_op | source)
XLA Modules:
  0.0 269.2 jit_solution(12242097150226354639)
XLA Ops:
  6.5 0.7 all-gather.5.cloned.1.call-update
  7.3 0.7 slice.28
  8.0 1.9 slice.29.source_ref
  9.9 3.3 %multiply_reduce_fusion = (f32[2048]{0:T(1024)S(1)}, bf16[2048,512]{1,0:T(8,128)(2,1)}) fusion(bf16[16384,512]{1,0:T(8,128)(2,1)} %param.4, s32[]{:T(128)S(6)} %select_n.22), kind=kLoop, calls=%fused_computation.2 | loop fusion | flops 3143680 | bytes 4202500 | tf_op jit(solution)/shard_map/reduce_sum | solution.py:149
  13.2 1.3 copy.25.center_norm_ref
  14.5 1.2 multiply_reduce_fusion.1
  15.8 0.9 copy.26.source_norm_ref
  16.6 45.3 %all-gather = bf16[512,512]{1,0:T(8,128)(2,1)S(1)} all-gather(bf16[16,512]{1,0:T(8,128)(2,1)S(1)} %slice.28), channel_id=2, replica_groups=mesh['frames'=32,'centers'=1] {'frames'}, dimensions={0}, use_global_device_ids=true | all-gather | bytes 540672 | tf_op jit(solution)/shard_map/all_gather | solution.py:160
  63.2 6.6 %all-gather.5.cloned.1.call-done.rows_ref = bf16[8192,512]{1,0:T(8,128)(2,1)} async-done(((bf16[1024,512]{1,0:T(8,128)(2,1)}), bf16[8192,512]{1,0:T(8,128)(2,1)}) %all-gather.5.cloned.1.call-update) | async-done | bytes 8388624 | tf_op jit(solution)/shard_map/all_gather | solution.py:161
  69.8 51.2 %members.1 = (bf16[2048,8192]{1,0:T(8,128)(2,1)}, bf16[512,8192]{1,0:T(8,128)(2,1)}, f32[1,8192]{1,0:T(1,128)}, f32[1,8192]{1,0:T(1,128)}, f32[1,8192]{1,0:T(1,1...) custom-call(bf16[8192,512]{1,0:T(8,128)(2,1)} %all-gather.5.cloned.1.call-done.rows_ref, ...), custom_call_target="tpu_custom_call" | custom-call | flops 21474836480 | bytes 50331648 | tf_op jit(solution)/shard_map/members/pallas_call | solution.py:73
  121.0 0.8 maximum_bitcast_fusion
  121.8 9.9 %all-gather.2 = f32[8,2,8320]{2,1,0:T(2,128)S(1)} all-gather(f32[1,2,8320]{2,1,0:T(2,128)S(1)} %maximum_bitcast_fusion), channel_id=3, replica_groups={{0,1,2,3,4,5,6,7},{8,9,10,11,12,13,14,15},{16,17,18,19,20,21,22,23},{24..., dimensions={0}, use_global_device_ids=true | all-gather | bytes 599040 | tf_op jit(solution)/shard_map/all_gather | solution.py:185
  132.2 0.9 maximum_reduce_fusion
  133.2 1.5 fusion.4
  134.7 24.3 %counts.1 = f32[512,2048]{1,0:T(8,128)} custom-call(bf16[512,8192]{1,0:T(8,128)(2,1)} %get-tuple-element.13.lead_ref, f32[1,8192]{1,0:T(1,128)} %bitcast.36, bf16[2048,8192]{1,0:T(8,128)(2,1)} %get-tuple-element.20.member_ref), custom_call_target="tpu_custom_call" | custom-call | flops 17179869184 | bytes 41943040 | tf_op jit(solution)/shard_map/counts/pallas_call | solution.py:124
  159.0 2.5 reduce_max.19
  161.5 2.6 multiply_convert_fusion
  164.8 57.2 %all_to_all.5 = f16[32,16,2176]{2,1,0:T(8,128)(2,1)S(1)} all-to-all(f16[32,16,2176]{2,1,0:T(8,128)(2,1)S(1)} %bitcast.32), channel_id=1, replica_groups=mesh['frames'=32,'centers'=1] {'frames'}, dimensions={0} | all-to-all | bytes 4456448 | tf_op jit(solution)/shard_map/all_to_all | solution.py:212
  221.9 13.7 %copy.28 = f16[32,16,2176]{0,1,2:T(8,128)(2,1)} copy(f16[32,16,2176]{2,1,0:T(8,128)(2,1)S(1)} %all_to_all.5) | data formatting | bytes 4456448 | tf_op jit(solution)/shard_map/all_to_all | solution.py:212
  235.7 4.8 %convert_element_type.32 = f32[32,16,2176]{0,1,2:T(8,128)S(1)} convert(f16[32,16,2176]{0,1,2:T(8,128)(2,1)} %copy.28) | non-fusion elementwise | flops 1114112 | bytes 6684672 | tf_op jit(solution)/shard_map/convert_element_type | solution.py:214
  240.5 6.1 %slice_multiply_fusion = f32[32,16,2048]{0,1,2:T(8,128)} fusion(f32[32,16,2176]{0,1,2:T(8,128)S(1)} %convert_element_type.32, f32[32,16]{0,1:T(8,128)S(1)} %fusion.14), kind=kLoop, calls=%fused_computation | loop fusion | flops 1048576 | bytes 8390656 | tf_op jit(solution)/shard_map/mul | solution.py:217
  246.6 12.0 %copy.29 = f32[32,16,2048]{2,1,0:T(8,128)} copy(f32[32,16,2048]{0,1,2:T(8,128)} %slice_multiply_fusion) | data formatting | bytes 8388608 | tf_op jit(solution)/shard_map/mul | solution.py:217
  258.6 2.6 reduce_sum.59
  261.3 1.1 copy.33
  (16 shorter events, 2.7 us)
Async XLA Ops:
  6.5 63.3 %all-gather.5.cloned.1.call-start = ((), (), s32[]{:S(2)}) async-start(), calls=%async_computation.1 | async-start | bytes 9437184 | tf_op jit(solution)/shard_map/all_gather | solution.py:161
  7.3 55.4 %copy-start = (s32[64]{0:T(128)S(1)}, s32[64]{0:T(128)}, u32[]{:S(2)}) copy-start(s32[64]{0:T(128)} %param.5) | copy-start | bytes 772
Sparse Core Ops, SparseCore 0:
  9.2 60.5 all-gather.4

commit v2 on v0

v2 whole, which is shorter than its diff:
```python
import functools
import math

import jax
import jax.numpy as jnp
from jax import lax
from jax.experimental import pallas as pl
from jax.experimental.pallas import tpu as pltpu
from jax.sharding import PartitionSpec as P

K = 16384
W = 512
LAG = 5
GROUP = 8
HALO = 128
TAIL = 16
TILE = 512
SHARPNESS = 0.03125
ALPHA = 2.0 * SHARPNESS * math.log2(math.e)
VMEM_BYTES = 56 * 1024 * 1024
TRANS_B = (((1,), (1,)), ((), ()))


COLUMN_TILES = 4
DEPTH_TILE = 2048
MESH = pl.DeviceIdType.MESH


def flipped(place, mask):
    bits = [(place // b + mask // b) % 2 for b in (1, 2, 4)]
    return bits[0] + 2 * bits[1] + 4 * bits[2]


def greet(peers):
    barrier = pltpu.get_barrier_semaphore()
    for peer in peers:
        pl.semaphore_signal(
            barrier, inc=1, device_id={"frames": peer}, device_id_type=MESH
        )
    pl.semaphore_wait(barrier, len(peers))


def half_norm_of(points):
    wide = points.astype(jnp.float32)
    return 0.5 * jnp.sum(wide * wide, axis=1, keepdims=True)


def weights_of(points, norms, rows):
    score = (
        lax.dot_general(points, rows, TRANS_B, preferred_element_type=jnp.float32) - norms
    )
    top = jnp.max(score, axis=0, keepdims=True)
    return top, jnp.exp2(ALPHA * (score - top))


def members_kernel(
    frames_ref, centers_ref, source_ref,
    member_ref, lead_ref, top_ref, sum_ref, lead_top_ref, halo_top_ref, halo_sum_ref, halo_lead_top_ref,
    rows, tail, halo, own, own_norm, source_norm, member_out, lead_out, halo_out,
    load_sem, out_sem, halo_sem, send_sem, recv_sem,
):
    devices = lax.axis_size("frames")
    me = lax.axis_index("frames")
    plane, place = me // GROUP, me % GROUP
    base = plane * GROUP
    near = {mask: base + flipped(place, mask) for mask in (1, 2, 4)}
    above = lax.rem(me + GROUP, devices)
    below = lax.rem(me + devices - GROUP, devices)
    states = own.shape[0]

    def part(mask, half):
        at = flipped(place, mask)
        return rows.at[pl.ds(pl.multiple_of(at * 2 * TILE + half * TILE, TILE), TILE), :]

    plan = [(mask, half, to) for half in (0, 1) for mask, to in ((0, 1), (0, 2), (0, 4))]
    plan += [(mask, half, 1) for half in (0, 1) for mask in (2, 4)]
    plan += [(4, 0, 2), (2, 1, 4), (6, 0, 1), (6, 1, 1)]
    copies = {}
    for number, (mask, half, to) in enumerate(plan):
        piece = part(mask, half)
        copies[mask, half, to] = pltpu.make_async_remote_copy(
            src_ref=piece, dst_ref=piece,
            send_sem=send_sem.at[number], recv_sem=recv_sem.at[number],
            device_id={"frames": near[to]}, device_id_type=MESH,
        )
    last = rows.shape[0] - TAIL
    tail_copy = pltpu.make_async_remote_copy(
        src_ref=rows.at[pl.ds(last, TAIL), :], dst_ref=tail,
        send_sem=send_sem.at[len(plan)], recv_sem=recv_sem.at[len(plan)],
        device_id={"frames": above}, device_id_type=MESH,
    )

    load_rows = pltpu.make_async_copy(
        frames_ref, rows.at[pl.ds(pl.multiple_of(place * 2 * TILE, TILE), 2 * TILE), :], load_sem.at[0]
    )
    load_own = pltpu.make_async_copy(
        centers_ref.at[pl.ds(pl.multiple_of(place * states, states), states), :], own, load_sem.at[1]
    )
    load_rows.start()
    load_own.start()
    greet([near[1], near[2], near[4], above, below])
    load_rows.wait()
    for half in (0, 1):
        for to in (2, 4, 1):
            copies[0, half, to].start()
    load_own.wait()
    own_norm[...] = half_norm_of(own[...])
    source_norm[...] = half_norm_of(source_ref[...])
    halo[...] = jnp.zeros_like(halo)

    arrivals = {
        2: [((0, 0, 1), [])],
        3: [((0, 1, 1), [])],
        4: [((0, 0, 2), [(2, 0, 1)])],
        5: [((0, 0, 4), [(4, 0, 1), (4, 0, 2)])],
        6: [((2, 0, 1), [])],
        7: [((4, 0, 1), [])],
        8: [((0, 1, 2), [(2, 1, 1), (2, 1, 4)])],
        9: [((0, 1, 4), [(4, 1, 1)])],
        10: [((2, 1, 1), [])],
        11: [((4, 1, 1), [])],
        12: [((4, 0, 2), [(6, 0, 1)])],
        13: [((2, 1, 4), [(6, 1, 1)])],
        14: [((6, 0, 1), [])],
        15: [((6, 1, 1), [])],
    }

    def member_copy(slot, at):
        return pltpu.make_async_copy(
            member_out.at[slot], member_ref.at[:, pl.ds(at, TILE)], out_sem.at[0, slot]
        )

    def lead_copy(slot, at):
        return pltpu.make_async_copy(
            lead_out.at[slot], lead_ref.at[:, pl.ds(at + HALO, TILE)], out_sem.at[1, slot]
        )

    def work(step, carry):
        for number, waits in arrivals.items():
            @pl.when(step == number)
            def _():
                for arrived, onward in waits:
                    copies[arrived].wait_recv()
                    for sent in onward:
                        copies[sent].start()
                if number == 15:
                    tail_copy.start()

        quarter, rest = step // 4, step % 4
        middle = ((quarter + 1) // 2) % 2
        half = middle * (quarter - 1) + (1 - middle) * (rest % 2)
        mask = middle * (2 + 2 * (rest % 2) + rest // 2) + (1 - middle) * (
            6 * (quarter // 3) + rest // 2
        )
        block = 2 * flipped(place, mask) + half
        at = pl.multiple_of(block * TILE, TILE)
        slot = step % 2

        @pl.when(step >= 2)
        def _():
            member_copy(slot, 0).wait()
            lead_copy(slot, 0).wait()

        x = rows[pl.ds(at, TILE), :]
        top, weight = weights_of(own[...], own_norm[...], x)
        top_ref[block] = top
        sum_ref[block] = jnp.sum(weight, axis=0, keepdims=True)
        member_out[slot] = weight.astype(jnp.bfloat16)
        member_copy(slot, at).start()
        top, weight = weights_of(source_ref[...], source_norm[...], x)
        lead_top_ref[block] = top
        lead_out[slot] = weight.astype(jnp.bfloat16)
        lead_copy(slot, at).start()
        return carry

    lax.fori_loop(0, 2 * GROUP, work, 0)

    tail_copy.wait_recv()
    halo[HALO - TAIL :, :] = tail[...]
    x = halo[...]
    top, weight = weights_of(own[...], own_norm[...], x)
    halo_top_ref[...] = top
    halo_sum_ref[...] = jnp.sum(weight, axis=0, keepdims=True)
    top, weight = weights_of(source_ref[...], source_norm[...], x)
    halo_lead_top_ref[...] = top
    halo_out[...] = weight.astype(jnp.bfloat16)
    halo_copy = pltpu.make_async_copy(halo_out, lead_ref.at[:, pl.ds(0, HALO)], halo_sem)
    halo_copy.start()
    for slot in (0, 1):
        member_copy(slot, 0).wait()
        lead_copy(slot, 0).wait()
    halo_copy.wait()
    for copy in copies.values():
        copy.wait_send()
    tail_copy.wait_send()


def members(frames, centers, source):
    frame_count, depth = frames.shape[0] * GROUP, frames.shape[1]
    states = centers.shape[0] // GROUP
    tiles = frame_count // TILE
    stat = jax.ShapeDtypeStruct((tiles, 1, TILE), jnp.float32)
    halo_stat = jax.ShapeDtypeStruct((1, HALO), jnp.float32)
    anywhere = pl.BlockSpec(memory_space=pl.ANY)
    held = pl.BlockSpec(memory_space=pltpu.VMEM)
    return pl.pallas_call(
        members_kernel,
        in_specs=[anywhere, anywhere, held],
        out_specs=[anywhere, anywhere] + [held] * 6,
        out_shape=[
            jax.ShapeDtypeStruct((states, frame_count), jnp.bfloat16),
            jax.ShapeDtypeStruct((W, frame_count + HALO), jnp.bfloat16),
            stat, stat, stat, halo_stat, halo_stat, halo_stat,
        ],
        scratch_shapes=[
            pltpu.VMEM((frame_count, depth), jnp.bfloat16),
            pltpu.VMEM((TAIL, depth), jnp.bfloat16),
            pltpu.VMEM((HALO, depth), jnp.bfloat16),
            pltpu.VMEM((states, depth), jnp.bfloat16),
            pltpu.VMEM((states, 1), jnp.float32),
            pltpu.VMEM((W, 1), jnp.float32),
            pltpu.VMEM((2, states, TILE), jnp.bfloat16),
            pltpu.VMEM((2, W, TILE), jnp.bfloat16),
            pltpu.VMEM((W, HALO), jnp.bfloat16),
            pltpu.SemaphoreType.DMA((2,)),
            pltpu.SemaphoreType.DMA((2, 2)),
            pltpu.SemaphoreType.DMA(()),
            pltpu.SemaphoreType.DMA((16,)),
            pltpu.SemaphoreType.DMA((16,)),
        ],
        compiler_params=pltpu.CompilerParams(
            vmem_limit_bytes=VMEM_BYTES, collective_id=0, has_side_effects=True
        ),
        cost_estimate=pl.CostEstimate(
            flops=2 * frame_count * depth * (states + W),
            bytes_accessed=2 * frame_count * (states + W + depth),
            transcendentals=frame_count * (states + W),
        ),
        name="members",
    )(frames, centers, source)


def counts_kernel(
    planes, factor, lead_ref, scale_ref, member_ref, out_ref,
    lead, slots, total, mine, sent, sent_unit, got, got_unit, summed,
    load_sem, send_sem, recv_sem, unit_send_sem, unit_recv_sem, own_sem, out_send_sem, out_recv_sem,
):
    me = lax.axis_index("frames")
    plane, place = me // GROUP, me % GROUP
    states, frame_count = member_ref.shape
    tile = states // COLUMN_TILES
    plane_rows = W // planes
    owned = plane_rows // GROUP
    planes_away = [lax.rem(plane + d, planes) for d in range(1, planes)]
    others = [plane * GROUP + lax.rem(place + d, GROUP) for d in range(1, GROUP)]

    def load(j, slot):
        return pltpu.make_async_copy(
            member_ref.at[pl.ds(pl.multiple_of(j * tile, tile), tile), :], slots.at[slot], load_sem.at[slot]
        )

    def exchange(j, d):
        to = {"frames": planes_away[d - 1] * GROUP + place}
        return [
            pltpu.make_async_remote_copy(
                src_ref=sent.at[j, d - 1], dst_ref=got.at[j, d - 1],
                send_sem=send_sem.at[j, d - 1], recv_sem=recv_sem.at[j, d - 1],
                device_id=to, device_id_type=MESH,
            ),
            pltpu.make_async_remote_copy(
                src_ref=sent_unit.at[j, d - 1], dst_ref=got_unit.at[j, d - 1],
                send_sem=unit_send_sem.at[j, d - 1], recv_sem=unit_recv_sem.at[j, d - 1],
                device_id=to, device_id_type=MESH,
            ),
        ]

    def columns(j):
        return out_ref.at[:, pl.ds(pl.multiple_of(place * states + j * tile, tile), tile)]

    def hand_out(j, d):
        to = lax.rem(place + d, GROUP)
        return pltpu.make_async_remote_copy(
            src_ref=summed.at[j, pl.ds(pl.multiple_of(to * owned, owned), owned), :], dst_ref=columns(j),
            send_sem=out_send_sem.at[j, d - 1], recv_sem=out_recv_sem.at[j, d - 1],
            device_id={"frames": others[d - 1]}, device_id_type=MESH,
        )

    def keep(j):
        return pltpu.make_async_copy(
            summed.at[j, pl.ds(pl.multiple_of(place * owned, owned), owned), :], columns(j), own_sem.at[j]
        )

    load(0, 0).start()
    greet([away * GROUP + place for away in planes_away] + others)

    def prepare(t, carry):
        at = pl.multiple_of(t * TILE, TILE)
        wide = lead_ref[:, pl.ds(at, TILE + HALO)].astype(jnp.float32)
        moved = pltpu.roll(wide, LAG, 1)[:, HALO:]
        lead[:, pl.ds(at, TILE)] = (moved * scale_ref[:, pl.ds(at, TILE)]).astype(jnp.bfloat16)
        return carry

    lax.fori_loop(0, frame_count // TILE, prepare, 0)

    def work(j, carry):
        slot = j % 2
        load(j, slot).wait()

        @pl.when(j + 1 < COLUMN_TILES)
        def _():
            load(j + 1, (j + 1) % 2).start()

        total[...] = jnp.zeros_like(total)

        def add(t, inner):
            at = pl.ds(pl.multiple_of(t * DEPTH_TILE, DEPTH_TILE), DEPTH_TILE)
            total[...] += lax.dot_general(
                lead[:, at], slots[slot, :, at], TRANS_B, preferred_element_type=jnp.float32
            )
            return inner

        lax.fori_loop(0, frame_count // DEPTH_TILE, add, 0)
        mine[j] = total[pl.ds(pl.multiple_of(plane * plane_rows, plane_rows), plane_rows), :]
        for d in range(1, planes):
            piece = total[
                pl.ds(pl.multiple_of(planes_away[d - 1] * plane_rows, plane_rows), plane_rows), :
            ]
            column_top = jnp.maximum(jnp.max(piece, axis=0, keepdims=True), 1e-30)
            coded = (piece * (32767.0 / column_top) + 0.5).astype(jnp.int32)
            sent[j, d - 1] = jnp.minimum(coded, 32767).astype(jnp.int16)
            sent_unit[j, d - 1] = jnp.broadcast_to(column_top * (factor / 32767.0), (8, tile))
            for copy in exchange(j, d):
                copy.start()
        return carry

    lax.fori_loop(0, COLUMN_TILES, work, 0)

    def finish(j, carry):
        value = mine[j] * factor
        for d in range(1, planes):
            for copy in exchange(j, d):
                copy.wait_recv()
            decoded = got[j, d - 1].astype(jnp.int32).astype(jnp.float32)
            value += decoded * got_unit[j, d - 1][:1, :]
        summed[j] = value
        keep(j).start()
        for d in range(1, GROUP):
            hand_out(j, d).start()
        return carry

    lax.fori_loop(0, COLUMN_TILES, finish, 0)

    def close(j, carry):
        for d in range(1, planes):
            for copy in exchange(j, d):
                copy.wait_send()
        keep(j).wait()
        for d in range(1, GROUP):
            hand_out(j, d).wait_send()
            arrived = lax.rem(place + GROUP - d, GROUP)
            landed = out_ref.at[:, pl.ds(pl.multiple_of(arrived * states + j * tile, tile), tile)]
            pltpu.make_async_remote_copy(
                src_ref=landed, dst_ref=landed,
                send_sem=out_send_sem.at[j, d - 1], recv_sem=out_recv_sem.at[j, d - 1],
                device_id={"frames": others[d - 1]}, device_id_type=MESH,
            ).wait_recv()
        return carry

    lax.fori_loop(0, COLUMN_TILES, close, 0)


def counts_of(lead, scale, member, planes):
    states, frame_count = member.shape
    tile = states // COLUMN_TILES
    plane_rows = W // planes
    owned = plane_rows // GROUP
    held = pl.BlockSpec(memory_space=pltpu.VMEM)
    anywhere = pl.BlockSpec(memory_space=pl.ANY)
    pair = (COLUMN_TILES, planes - 1)
    return pl.pallas_call(
        functools.partial(counts_kernel, planes, K * K / (frame_count * planes)),
        in_specs=[held, held, anywhere],
        out_specs=anywhere,
        out_shape=jax.ShapeDtypeStruct((owned, GROUP * states), jnp.float32),
        scratch_shapes=[
            pltpu.VMEM((W, frame_count), jnp.bfloat16),
            pltpu.VMEM((2, tile, frame_count), jnp.bfloat16),
            pltpu.VMEM((W, tile), jnp.float32),
            pltpu.VMEM((COLUMN_TILES, plane_rows, tile), jnp.float32),
            pltpu.VMEM(pair + (plane_rows, tile), jnp.int16),
            pltpu.VMEM(pair + (8, tile), jnp.float32),
            pltpu.VMEM(pair + (plane_rows, tile), jnp.int16),
            pltpu.VMEM(pair + (8, tile), jnp.float32),
            pltpu.VMEM((COLUMN_TILES, plane_rows, tile), jnp.float32),
            pltpu.SemaphoreType.DMA((2,)),
            pltpu.SemaphoreType.DMA(pair),
            pltpu.SemaphoreType.DMA(pair),
            pltpu.SemaphoreType.DMA(pair),
            pltpu.SemaphoreType.DMA(pair),
            pltpu.SemaphoreType.DMA((COLUMN_TILES,)),
            pltpu.SemaphoreType.DMA((COLUMN_TILES, GROUP - 1)),
            pltpu.SemaphoreType.DMA((COLUMN_TILES, GROUP - 1)),
        ],
        compiler_params=pltpu.CompilerParams(
            vmem_limit_bytes=VMEM_BYTES, collective_id=1, has_side_effects=True
        ),
        cost_estimate=pl.CostEstimate(
            flops=2 * frame_count * W * states,
            bytes_accessed=2 * frame_count * (states + W),
            transcendentals=0,
        ),
        name="counts",
    )(lead, scale, member)


def segment_of(positions, starts):
    return jnp.sum((starts[:, None] <= positions[None, :]).astype(jnp.int32), axis=0)


def shards(frames, centers, starts):
    devices = lax.axis_size("frames")
    planes = devices // GROUP
    plane = lax.axis_index("frames") // GROUP
    groups = [[p * GROUP + c for c in range(GROUP)] for p in range(planes)]

    source = centers[:W]
    if lax.axis_size("centers") > 1:
        mine = lax.axis_index("centers") == 0
        source = lax.psum(jnp.where(mine, source, jnp.zeros_like(source)), "centers")

    member, lead, top, total, lead_top, halo_top, halo_total, halo_lead_top = members(
        frames, centers, source
    )
    plane_frames = member.shape[1]
    top, total, lead_top = (v.reshape(1, plane_frames) for v in (top, total, lead_top))

    stats = jnp.concatenate(
        [
            jnp.concatenate([halo_top, top], axis=1),
            jnp.concatenate([halo_total, total], axis=1),
        ],
        axis=0,
    )
    gathered = lax.all_gather(stats, "frames", axis_index_groups=groups)
    all_top = lax.pmax(jnp.max(gathered[:, 0], axis=0), "centers")
    all_total = lax.psum(
        jnp.sum(gathered[:, 1] * jnp.exp2(ALPHA * (gathered[:, 0] - all_top)), axis=0),
        "centers",
    )

    positions = plane * plane_frames - HALO + jnp.arange(plane_frames + HALO, dtype=jnp.int32)
    usable = jnp.logical_and(
        segment_of(positions, starts) == segment_of(positions + LAG, starts),
        jnp.logical_and(positions >= 0, positions + LAG < plane_frames * planes),
    )
    lead_tops = jnp.concatenate([halo_lead_top, lead_top], axis=1)[0]
    lead_factor = jnp.where(usable, jnp.exp2(ALPHA * (lead_tops - all_top)) / all_total, 0.0)
    lag_factor = jnp.exp2(ALPHA * (top[0] - all_top[HALO:])) / all_total[HALO:]
    scale = lead_factor[HALO - LAG : HALO - LAG + plane_frames] * lag_factor

    return counts_of(lead, scale[None, :], member, planes)


def solution(mesh):
    return jax.shard_map(
        shards,
        mesh=mesh,
        in_specs=(P("frames", None), P("centers", None), P()),
        out_specs=P("frames", "centers"),
        check_vma=False,
    )
```

time: 523 us -> 145 us (0.28)
  blocking collectives: 371 us -> 9.57 us
  Pallas kernels: 0 us -> 127 us
  other arithmetic: 67.8 us -> 2.99 us
  matrix products: 57.8 us -> 0 us
  local copies, waits for them, and re-layouts: 24.3 us -> 4.15 us
    all_to_all x1 -> x0, blocking collectives: 371 us -> none  [shards(): lax.all_to_all(pieces.astype(jnp.bfloat16), 'frames', split_axis=0, conca...]
    pallas_call x0 -> x2, Pallas kernels: none -> 127 us  [the longest x1 69.9 us: counts_of(): pl.pallas_call(functools.partial(counts_kernel, planes, K * K / (frame_co...]
    dot_general x2 -> x0, matrix products: 57.8 us -> none  [the longest x1 31.9 us: logits_of(): lax.dot_general(row_block, centers, (((1,), (1,)), ((), ())), preferred_e...]
    convert_element_type x2 -> x0, other arithmetic: 33.5 us -> none  [the longest x1 33.5 us: shards(): member = (exponent / row_total[:, None]).astype(jnp.bfloat16)]
    reduce_sum x5 -> x2, other arithmetic: 33.3 us -> 0.74 us  [the longest x1 0.6 us: segment_of(): jnp.sum((starts[:, None] <= positions[None, :]).astype(jnp.int32), axis=0)]
    slice x2 -> x1, local copies, waits for them, and re-layouts: 24.3 us -> 1.87 us  [shards(): source = centers[:W]]
    all_gather x0 -> x1, blocking collectives: none -> 9.57 us  [shards(): gathered = lax.all_gather(stats, 'frames', axis_index_groups=groups)]
  transfers between devices with their start and end apart: 1 -> 0, of which waited for: 0 -> 0; matrix products, arithmetic and copies ran while one was open for 4% -> 0% of each run, Pallas kernels for 0% -> 0%
where the time goes in v2:
time: 145 us; the launch traced here: 144 us
  Pallas kernels  127 us (88%)
  blocking collectives  9.57 us (7%)
  local copies, waits for them, and re-layouts  4.15 us (3%)
  other arithmetic  2.99 us (2%)
    pallas_call x1, Pallas kernels, counts_of(): pl.pallas_call(functools.partial(counts_kernel, planes, K * K / (frame_co...  69.9 us
    pallas_call x1, Pallas kernels, members(): pl.pallas_call(members_kernel, in_specs=[anywhere, anywhere, held], out_s...  56.8 us
    all_gather x1, blocking collectives, shards(): gathered = lax.all_gather(stats, 'frames', axis_index_groups=groups)  9.57 us

profile of v2, /device:TPU:0, one launch (start us, length us, event | category | flops | bytes accessed | tf_op | source)
XLA Modules:
  0.0 143.5 jit_solution(8157335592454581982)
XLA Ops:
  0.0 1.9 %slice.19.source_ref = bf16[512,512]{1,0:T(8,128)(2,1)} slice(bf16[16384,512]{1,0:T(8,128)(2,1)} %centers_ref.1), slice={[0:512], [0:512]} | slice | bytes 1048576 | tf_op jit(solution)/shard_map/slice | solution.py:426
  1.9 56.8 %members.1 = (bf16[2048,8192]{1,0:T(8,128)(2,1)}, bf16[512,8320]{1,0:T(8,128)(2,1)}, f32[16,1,512]{2,1,0:T(1,128)}, f32[16,1,512]{2,1,0:T(1,128)}, f32[16,1,512]...) custom-call(bf16[1024,512]{1,0:T(8,128)(2,1)} %frames_ref.1, ...), custom_call_target="tpu_custom_call" | custom-call | flops 21474836480 | bytes 50331648 | tf_op jit(solution)/shard_map/members/pallas_call | solution.py:206
  58.7 0.0 copy-start.2
  58.7 0.0 copy-start.1
  58.7 0.0 copy-start.3
  58.7 0.0 copy-start
  58.7 0.9 maximum_bitcast_fusion
  59.6 9.6 %all-gather.1 = f32[8,2,8320]{2,1,0:T(2,128)S(1)} all-gather(f32[1,2,8320]{2,1,0:T(2,128)S(1)} %maximum_bitcast_fusion), channel_id=2, replica_groups={{0,1,2,3,4,5,6,7},{8,9,10,11,12,13,14,15},{16,17,18,19,20,21,22,23},{24..., dimensions={0}, use_global_device_ids=true | all-gather | bytes 599040 | tf_op jit(solution)/shard_map/all_gather | solution.py:444
  69.2 0.5 slice_reduce_fusion
  69.7 0.1 fusion.1
  69.9 0.0 copy-done.2
  69.9 0.6 convert_reduce_fusion.1
  70.5 0.0 copy-done.1
  70.5 0.0 copy-done.3
  70.5 0.1 maximum_reduce_fusion
  70.6 0.0 copy-done
  70.6 0.8 fusion.4
  71.4 69.9 %counts.1 = f32[16,16384]{1,0:T(8,128)} custom-call(bf16[512,8320]{1,0:T(8,128)(2,1)} %get-tuple-element.13.lead_ref, f32[1,8192]{1,0:T(1,128)} %bitcast.25, bf16[2048,8192]{1,0:T(8,128)(2,1)} %get-tuple-element.20.member_ref), custom_call_target="tpu_custom_call" | custom-call | flops 17179869184 | bytes 41943040 | tf_op jit(solution)/shard_map/counts/pallas_call | solution.py:380
  141.3 2.3 %copy.16 = f32[16,16384]{1,0:T(8,128)} copy(f32[16,16384]{1,0:T(8,128)} %counts.1) | data formatting | bytes 2097152
  (1 shorter events, 0.0 us)
Async XLA Ops:
  58.7 11.2 %copy-start.2 = (s32[64]{0:T(128)S(1)}, s32[64]{0:T(128)}, u32[]{:S(2)}) copy-start(s32[64]{0:T(128)} %param.5) | copy-start | bytes 772
  58.7 11.8 %copy-start.1 = (f32[16,1,512]{2,1,0:T(1,128)S(1)}, f32[16,1,512]{2,1,0:T(1,128)}, u32[]{:S(2)}) copy-start(f32[16,1,512]{2,1,0:T(1,128)} %get-tuple-element.15) | copy-start | bytes 98308
  58.7 11.8 %copy-start.3 = (f32[1,128]{1,0:T(1,128)S(1)}, f32[1,128]{1,0:T(1,128)}, u32[]{:S(2)}) copy-start(f32[1,128]{1,0:T(1,128)} %get-tuple-element.14) | copy-start | bytes 1540
  58.7 11.9 %copy-start = (f32[16,1,512]{2,1,0:T(1,128)S(1)}, f32[16,1,512]{2,1,0:T(1,128)}, u32[]{:S(2)}) copy-start(f32[16,1,512]{2,1,0:T(1,128)} %get-tuple-element.17) | copy-start | bytes 98308

commit v3 on v2

v3 whole, which is shorter than its diff:
```python
import functools
import math

import jax
import jax.numpy as jnp
from jax import lax
from jax.experimental import pallas as pl
from jax.experimental.pallas import tpu as pltpu
from jax.sharding import PartitionSpec as P

K = 16384
W = 512
LAG = 5
GROUP = 8
HALO = 128
TAIL = 16
TILE = 512
SHARPNESS = 0.03125
ALPHA = 2.0 * SHARPNESS * math.log2(math.e)
VMEM_BYTES = 56 * 1024 * 1024
TRANS_B = (((1,), (1,)), ((), ()))


COLUMN_TILES = 8
CHUNK = 256
DEPTH_TILE = 2048
MESH = pl.DeviceIdType.MESH


def flipped(place, mask):
    bits = [(place // b + mask // b) % 2 for b in (1, 2, 4)]
    return bits[0] + 2 * bits[1] + 4 * bits[2]


def placed(index):
    return index // 16, (index // 4) % 2, (index // 8) % 2 * 4 + index % 4


def device_at(outer, row, place):
    return outer * 16 + place // 4 * 8 + row * 4 + place % 4


def greet(peers):
    barrier = pltpu.get_barrier_semaphore()
    for peer in peers:
        pl.semaphore_signal(
            barrier, inc=1, device_id={"frames": peer}, device_id_type=MESH
        )
    pl.semaphore_wait(barrier, len(peers))


def folded(values, combine):
    return combine(values.reshape(values.shape[0] // 8, 8, values.shape[1]), axis=0)


def members_kernel(
    frames_ref, centers_ref, source_ref,
    member_ref, lead_ref, top_ref, sum_ref, lead_top_ref, halo_top_ref, halo_sum_ref, halo_lead_top_ref,
    rows, tail, halo, points, norms, score_even, score_odd, member_out, lead_out, halo_out,
    load_sem, out_sem, halo_sem, send_sem, recv_sem, tail_send_sem, tail_recv_sem,
):
    outers = lax.axis_size("frames") // 16
    outer, row, place = placed(lax.axis_index("frames"))
    near = {mask: device_at(outer, row, flipped(place, mask)) for mask in (1, 2, 4)}
    beside = device_at(outer, 1 - row, place)
    across = device_at(lax.rem(outer + 2 * row - 1 + outers, outers), 1 - row, place)
    follows = device_at(lax.rem(outer + row, outers), 1 - row, place)
    states = points.shape[0] - W

    def part(mask, half):
        at = flipped(place, mask)
        return rows.at[pl.ds(pl.multiple_of(at * 2 * TILE + half * TILE, TILE), TILE), :]

    plan = [(mask, half, to) for half in (0, 1) for mask, to in ((0, 1), (0, 2), (0, 4))]
    plan += [(mask, half, 1) for half in (0, 1) for mask in (2, 4)]
    plan += [(4, 0, 2), (2, 1, 4), (6, 0, 1), (6, 1, 1)]
    copies = {}
    for number, (mask, half, to) in enumerate(plan):
        piece = part(mask, half)
        copies[mask, half, to] = pltpu.make_async_remote_copy(
            src_ref=piece, dst_ref=piece,
            send_sem=send_sem.at[number], recv_sem=recv_sem.at[number],
            device_id={"frames": near[to]}, device_id_type=MESH,
        )
    run = rows.shape[0] // 2

    def tail_copy(number, slot, to):
        return pltpu.make_async_remote_copy(
            src_ref=rows.at[pl.ds((number + 1) * run - TAIL, TAIL), :], dst_ref=tail.at[slot],
            send_sem=tail_send_sem.at[number], recv_sem=tail_recv_sem.at[slot],
            device_id={"frames": to}, device_id_type=MESH,
        )

    tails = [tail_copy(0, row, beside), tail_copy(1, 1 - row, follows)]

    load_rows = pltpu.make_async_copy(
        frames_ref, rows.at[pl.ds(pl.multiple_of(place * 2 * TILE, TILE), 2 * TILE), :], load_sem.at[0]
    )
    load_own = pltpu.make_async_copy(
        centers_ref.at[pl.ds(pl.multiple_of(place * states, states), states), :], points.at[pl.ds(0, states), :], load_sem.at[1]
    )
    load_source = pltpu.make_async_copy(source_ref, points.at[pl.ds(states, W), :], load_sem.at[2])
    load_rows.start()
    load_own.start()
    load_source.start()
    greet([near[1], near[2], near[4], beside, across])
    load_rows.wait()
    for half in (0, 1):
        for to in (2, 4, 1):
            copies[0, half, to].start()
    load_own.wait()
    load_source.wait()

    def square(n, carry):
        at = pl.ds(pl.multiple_of(n * CHUNK, CHUNK), CHUNK)
        wide = points[at, :].astype(jnp.float32)
        norm = 0.5 * jnp.sum(wide * wide, axis=1, keepdims=True)
        norms[at, :] = jnp.broadcast_to(norm, (CHUNK, 128))
        return carry

    lax.fori_loop(0, (states + W) // CHUNK, square, 0)
    halo[...] = jnp.zeros_like(halo)

    arrivals = {
        2: [((0, 0, 1), [])],
        3: [((0, 1, 1), [])],
        4: [((0, 0, 2), [(2, 0, 1)])],
        5: [((0, 0, 4), [(4, 0, 1), (4, 0, 2)])],
        6: [((2, 0, 1), [])],
        7: [((4, 0, 1), [])],
        8: [((0, 1, 2), [(2, 1, 1), (2, 1, 4)])],
        9: [((0, 1, 4), [(4, 1, 1)])],
        10: [((2, 1, 1), [])],
        11: [((4, 1, 1), [])],
        12: [((4, 0, 2), [(6, 0, 1)])],
        13: [((2, 1, 4), [(6, 1, 1)])],
        14: [((6, 0, 1), [])],
        15: [((6, 1, 1), [])],
    }

    def member_copy(slot, at):
        return pltpu.make_async_copy(
            member_out.at[slot], member_ref.at[:, pl.ds(at, TILE)], out_sem.at[0, slot]
        )

    def lead_copy(slot, at):
        return pltpu.make_async_copy(
            lead_out.at[slot], lead_ref.at[:, pl.ds(at, TILE)], out_sem.at[1, slot]
        )

    def arrive(step):
        for number, waits in arrivals.items():
            @pl.when(step == number)
            def _():
                for arrived, onward in waits:
                    copies[arrived].wait_recv()
                    for sent in onward:
                        copies[sent].start()
                if number == 15:
                    for copy in tails:
                        copy.start()

    def block_at(step):
        quarter, rest = step // 4, step % 4
        middle = ((quarter + 1) // 2) % 2
        half = middle * (quarter - 1) + (1 - middle) * (rest % 2)
        mask = middle * (2 + 2 * (rest % 2) + rest // 2) + (1 - middle) * (
            6 * (quarter // 3) + rest // 2
        )
        return 2 * flipped(place, mask) + half

    scores = (score_even, score_odd)

    def passes(x, score, done, tops, member_at, lead_at):
        best = [None, None]
        sums = None
        for n in range((states + W) // CHUNK):
            kind = int(n * CHUNK >= states)
            at = slice(n * CHUNK, (n + 1) * CHUNK)
            if x is not None:
                norm = jnp.concatenate([norms[at, :]] * (x.shape[0] // 128), axis=1)
                value = (
                    lax.dot_general(points[at, :], x, TRANS_B, preferred_element_type=jnp.float32)
                    - norm
                )
                score[at, : x.shape[0]] = value
                top = folded(value, jnp.max)
                best[kind] = top if best[kind] is None else jnp.maximum(best[kind], top)
            if done is not None:
                width = tops[kind].shape[1]
                weight = jnp.exp2(ALPHA * (done[at, :width] - tops[kind]))
                if kind == 0:
                    if member_at is not None:
                        member_at[at, :] = weight.astype(jnp.bfloat16)
                    part_sum = folded(weight, jnp.sum)
                    sums = part_sum if sums is None else sums + part_sum
                else:
                    lead_at[n * CHUNK - states : (n + 1) * CHUNK - states, :] = weight.astype(
                        jnp.bfloat16
                    )
        if x is not None:
            best = tuple(jnp.max(b, axis=0, keepdims=True) for b in best)
        if done is not None:
            sums = jnp.sum(sums, axis=0, keepdims=True)
        return best, sums

    def rows_at(block):
        return rows[pl.ds(pl.multiple_of(block * TILE, TILE), TILE), :]

    def turn(step, slot, tops, more=True):
        block = block_at(step)
        x = None
        if more:
            arrive(step + 1)
            x = rows_at(block_at(step + 1))

        @pl.when(step >= 2)
        def _():
            member_copy(slot, 0).wait()
            lead_copy(slot, 0).wait()

        following, sums = passes(
            x, scores[1 - slot], scores[slot], tops, member_out.at[slot], lead_out.at[slot]
        )
        top_ref[block] = tops[0]
        lead_top_ref[block] = tops[1]
        sum_ref[block] = sums
        at = pl.multiple_of(block * TILE, TILE)
        member_copy(slot, at).start()
        lead_copy(slot, pl.multiple_of(at + HALO * (1 + block // GROUP), 128)).start()
        return following

    def work(pair, tops):
        tops = turn(2 * pair, 0, tops)
        return turn(2 * pair + 1, 1, tops)

    tops, _ = passes(rows_at(block_at(jnp.int32(0))), score_even, None, None, None, None)
    tops = lax.fori_loop(0, GROUP - 1, work, tops)
    tops = turn(jnp.int32(2 * GROUP - 2), 0, tops)
    turn(jnp.int32(2 * GROUP - 1), 1, tops, more=False)

    for slot in (0, 1):
        tail_copy(0, slot, beside).wait_recv()
        halo[(slot + 1) * HALO - TAIL : (slot + 1) * HALO, :] = tail[slot]
    tops, _ = passes(halo[...], score_even, None, None, None, None)
    _, sums = passes(None, None, score_even, tops, None, halo_out)
    halo_top_ref[...] = tops[0]
    halo_sum_ref[...] = sums
    halo_lead_top_ref[...] = tops[1]
    halo_copies = [
        pltpu.make_async_copy(
            halo_out.at[:, pl.ds(slot * HALO, HALO)],
            lead_ref.at[:, pl.ds(slot * (HALO + run), HALO)],
            halo_sem.at[slot],
        )
        for slot in (0, 1)
    ]
    for copy in halo_copies:
        copy.start()
    for slot in (0, 1):
        member_copy(slot, 0).wait()
        lead_copy(slot, 0).wait()
    for copy in halo_copies:
        copy.wait()
    for copy in copies.values():
        copy.wait_send()
    for copy in tails:
        copy.wait_send()


def members(frames, centers, source):
    frame_count, depth = frames.shape[0] * GROUP, frames.shape[1]
    states = centers.shape[0] // GROUP
    tiles = frame_count // TILE
    stat = jax.ShapeDtypeStruct((tiles, 1, TILE), jnp.float32)
    halo_stat = jax.ShapeDtypeStruct((1, 2 * HALO), jnp.float32)
    anywhere = pl.BlockSpec(memory_space=pl.ANY)
    held = pl.BlockSpec(memory_space=pltpu.VMEM)
    return pl.pallas_call(
        members_kernel,
        in_specs=[anywhere, anywhere, anywhere],
        out_specs=[anywhere, anywhere] + [held] * 6,
        out_shape=[
            jax.ShapeDtypeStruct((states, frame_count), jnp.bfloat16),
            jax.ShapeDtypeStruct((W, frame_count + 2 * HALO), jnp.bfloat16),
            stat, stat, stat, halo_stat, halo_stat, halo_stat,
        ],
        scratch_shapes=[
            pltpu.VMEM((frame_count, depth), jnp.bfloat16),
            pltpu.VMEM((2, TAIL, depth), jnp.bfloat16),
            pltpu.VMEM((2 * HALO, depth), jnp.bfloat16),
            pltpu.VMEM((states + W, depth), jnp.bfloat16),
            pltpu.VMEM((states + W, 128), jnp.float32),
            pltpu.VMEM((states + W, TILE), jnp.float32),
            pltpu.VMEM((states + W, TILE), jnp.float32),
            pltpu.VMEM((2, states, TILE), jnp.bfloat16),
            pltpu.VMEM((2, W, TILE), jnp.bfloat16),
            pltpu.VMEM((W, 2 * HALO), jnp.bfloat16),
            pltpu.SemaphoreType.DMA((3,)),
            pltpu.SemaphoreType.DMA((2, 2)),
            pltpu.SemaphoreType.DMA((2,)),
            pltpu.SemaphoreType.DMA((16,)),
            pltpu.SemaphoreType.DMA((16,)),
            pltpu.SemaphoreType.DMA((2,)),
            pltpu.SemaphoreType.DMA((2,)),
        ],
        compiler_params=pltpu.CompilerParams(
            vmem_limit_bytes=VMEM_BYTES, collective_id=0, has_side_effects=True
        ),
        cost_estimate=pl.CostEstimate(
            flops=2 * frame_count * depth * (states + W),
            bytes_accessed=2 * frame_count * (states + W + depth),
            transcendentals=frame_count * (states + W),
        ),
        name="members",
    )(frames, centers, source)


def coded(piece, factor):
    column_top = jnp.maximum(jnp.max(piece, axis=0, keepdims=True), 1e-30)
    steps = (piece * (32767.0 / column_top) + 0.5).astype(jnp.int32)
    unit = jnp.broadcast_to(column_top * (factor / 32767.0), (8, piece.shape[1]))
    return jnp.minimum(steps, 32767).astype(jnp.int16), unit


def decoded(steps, unit):
    return steps.astype(jnp.int32).astype(jnp.float32) * unit[:1, :]


def counts_kernel(
    outers, factor, lead_ref, scale_ref, member_ref, out_ref,
    lead, slots, total, half, half_sent, half_unit, half_got, half_got_unit,
    mine, sent, sent_unit, got, got_unit, summed,
    load_sem, half_sem, send_sem, recv_sem, unit_send_sem, unit_recv_sem, own_sem, out_send_sem, out_recv_sem,
):
    outer, row, place = placed(lax.axis_index("frames"))
    states, frame_count = member_ref.shape
    tile = max(128, states // COLUMN_TILES)
    tiles = states // tile
    outer_rows = W // 2 // outers
    owned = outer_rows // GROUP
    beside = device_at(outer, 1 - row, place)
    outers_away = [lax.rem(outer + d, outers) for d in range(1, outers)]
    others = [device_at(outer, row, lax.rem(place + d, GROUP)) for d in range(1, GROUP)]

    def load(j, slot):
        return pltpu.make_async_copy(
            member_ref.at[pl.ds(pl.multiple_of(j * tile, tile), tile), :], slots.at[slot], load_sem.at[slot]
        )

    def remote(source, target, send, recv, to):
        return pltpu.make_async_remote_copy(
            src_ref=source, dst_ref=target, send_sem=send, recv_sem=recv,
            device_id={"frames": to}, device_id_type=MESH,
        )

    def halves(j):
        return [
            remote(half_sent.at[j], half_got.at[j], half_sem.at[0, j], half_sem.at[1, j], beside),
            remote(half_unit.at[j], half_got_unit.at[j], half_sem.at[2, j], half_sem.at[3, j], beside),
        ]

    def exchange(j, d):
        to = device_at(outers_away[d - 1], row, place)
        at = (j, d - 1)
        return [
            remote(sent.at[at], got.at[at], send_sem.at[at], recv_sem.at[at], to),
            remote(sent_unit.at[at], got_unit.at[at], unit_send_sem.at[at], unit_recv_sem.at[at], to),
        ]

    def columns(j, whose):
        return out_ref.at[:, pl.ds(pl.multiple_of(whose * states + j * tile, tile), tile)]

    def hand_out(j, d):
        to = lax.rem(place + d, GROUP)
        return remote(
            summed.at[j, pl.ds(pl.multiple_of(to * owned, owned), owned), :], columns(j, place),
            out_send_sem.at[j, d - 1], out_recv_sem.at[j, d - 1], others[d - 1],
        )

    def keep(j):
        return pltpu.make_async_copy(
            summed.at[j, pl.ds(pl.multiple_of(place * owned, owned), owned), :], columns(j, place), own_sem.at[j]
        )

    load(0, 0).start()
    greet([beside] + [device_at(away, row, place) for away in outers_away] + others)

    def prepare(t, carry):
        at = pl.multiple_of(t * TILE, TILE)
        before = pl.multiple_of(at + HALO * (t // GROUP), 128)
        wide = lead_ref[:, pl.ds(before, TILE + HALO)].astype(jnp.float32)
        moved = pltpu.roll(wide, LAG, 1)[:, HALO:]
        lead[:, pl.ds(at, TILE)] = (moved * scale_ref[:, pl.ds(at, TILE)]).astype(jnp.bfloat16)
        return carry

    lax.fori_loop(0, frame_count // TILE, prepare, 0)

    def compute(j):
        slot = j % 2
        load(j, slot).wait()

        @pl.when(j + 1 < tiles)
        def _():
            load(j + 1, (j + 1) % 2).start()

        total[...] = jnp.zeros_like(total)

        def add(t, inner):
            at = pl.ds(pl.multiple_of(t * DEPTH_TILE, DEPTH_TILE), DEPTH_TILE)
            total[...] += lax.dot_general(
                lead[:, at], slots[slot, :, at], TRANS_B, preferred_element_type=jnp.float32
            )
            return inner

        lax.fori_loop(0, frame_count // DEPTH_TILE, add, 0)
        half_sent[j], half_unit[j] = coded(
            total[pl.ds(pl.multiple_of((1 - row) * (W // 2), W // 2), W // 2), :], 1.0
        )
        for copy in halves(j):
            copy.start()
        half[j] = total[pl.ds(pl.multiple_of(row * (W // 2), W // 2), W // 2), :]

    def merge(j):
        for copy in halves(j):
            copy.wait_recv()
        half[j] += decoded(half_got[j], half_got_unit[j])
        for d in range(1, outers):
            at = pl.multiple_of(outers_away[d - 1] * outer_rows, outer_rows)
            sent[j, d - 1], sent_unit[j, d - 1] = coded(half[j, pl.ds(at, outer_rows), :], factor)
            for copy in exchange(j, d):
                copy.start()
        mine[j] = half[j, pl.ds(pl.multiple_of(outer * outer_rows, outer_rows), outer_rows), :]

    def finish(j):
        value = mine[j] * factor
        for d in range(1, outers):
            for copy in exchange(j, d):
                copy.wait_recv()
            value += decoded(got[j, d - 1], got_unit[j, d - 1])
        summed[j] = value
        keep(j).start()
        for d in range(1, GROUP):
            hand_out(j, d).start()

    def work(step, carry):
        pl.when(step < tiles)(lambda: compute(step))
        pl.when(jnp.logical_and(step >= 2, step < tiles + 2))(lambda: merge(step - 2))
        pl.when(step >= 5)(lambda: finish(step - 5))
        return carry

    lax.fori_loop(0, tiles + 5, work, 0)

    def close(j, carry):
        for copy in halves(j):
            copy.wait_send()
        for d in range(1, outers):
            for copy in exchange(j, d):
                copy.wait_send()
        keep(j).wait()
        for d in range(1, GROUP):
            hand_out(j, d).wait_send()
            landed = columns(j, lax.rem(place + GROUP - d, GROUP))
            remote(
                landed, landed, out_send_sem.at[j, d - 1], out_recv_sem.at[j, d - 1], others[d - 1]
            ).wait_recv()
        return carry

    lax.fori_loop(0, tiles, close, 0)


def counts_of(lead, scale, member, outers):
    states, frame_count = member.shape
    tile = max(128, states // COLUMN_TILES)
    tiles = states // tile
    outer_rows = W // 2 // outers
    owned = outer_rows // GROUP
    held = pl.BlockSpec(memory_space=pltpu.VMEM)
    anywhere = pl.BlockSpec(memory_space=pl.ANY)
    pair = (tiles, outers - 1)
    return pl.pallas_call(
        functools.partial(counts_kernel, outers, K * K / (2 * frame_count * outers)),
        in_specs=[held, held, anywhere],
        out_specs=anywhere,
        out_shape=jax.ShapeDtypeStruct((owned, GROUP * states), jnp.float32),
        scratch_shapes=[
            pltpu.VMEM((W, frame_count), jnp.bfloat16),
            pltpu.VMEM((2, tile, frame_count), jnp.bfloat16),
            pltpu.VMEM((W, tile), jnp.float32),
            pltpu.VMEM((tiles, W // 2, tile), jnp.float32),
            pltpu.VMEM((tiles, W // 2, tile), jnp.int16),
            pltpu.VMEM((tiles, 8, tile), jnp.float32),
            pltpu.VMEM((tiles, W // 2, tile), jnp.int16),
            pltpu.VMEM((tiles, 8, tile), jnp.float32),
            pltpu.VMEM((tiles, outer_rows, tile), jnp.float32),
            pltpu.VMEM(pair + (outer_rows, tile), jnp.int16),
            pltpu.VMEM(pair + (8, tile), jnp.float32),
            pltpu.VMEM(pair + (outer_rows, tile), jnp.int16),
            pltpu.VMEM(pair + (8, tile), jnp.float32),
            pltpu.VMEM((tiles, outer_rows, tile), jnp.float32),
            pltpu.SemaphoreType.DMA((2,)),
            pltpu.SemaphoreType.DMA((4, tiles)),
            pltpu.SemaphoreType.DMA(pair),
            pltpu.SemaphoreType.DMA(pair),
            pltpu.SemaphoreType.DMA(pair),
            pltpu.SemaphoreType.DMA(pair),
            pltpu.SemaphoreType.DMA((tiles,)),
            pltpu.SemaphoreType.DMA((tiles, GROUP - 1)),
            pltpu.SemaphoreType.DMA((tiles, GROUP - 1)),
        ],
        compiler_params=pltpu.CompilerParams(
            vmem_limit_bytes=VMEM_BYTES, collective_id=1, has_side_effects=True
        ),
        cost_estimate=pl.CostEstimate(
            flops=2 * frame_count * W * states,
            bytes_accessed=2 * frame_count * (states + W),
            transcendentals=0,
        ),
        name="counts",
    )(lead, scale, member)


def segment_of(positions, starts):
    return jnp.sum((starts[:, None] <= positions[None, :]).astype(jnp.int32), axis=0)


def shards(frames, centers, starts):
    devices = lax.axis_size("frames")
    outers = devices // 16
    outer, row, _ = placed(lax.axis_index("frames"))
    groups = [[device_at(o, r, p) for p in range(GROUP)] for o in range(outers) for r in (0, 1)]

    source = centers[:W]
    if lax.axis_size("centers") > 1:
        mine = lax.axis_index("centers") == 0
        source = lax.psum(jnp.where(mine, source, jnp.zeros_like(source)), "centers")
    source = source.reshape(outers, 2, 2, -1, source.shape[1]).transpose(2, 0, 1, 3, 4)
    source = source.reshape(W, -1)

    member, lead, top, total, lead_top, halo_top, halo_total, halo_lead_top = members(
        frames, centers, source
    )
    group_frames = member.shape[1]
    run = group_frames // 2

    def with_halos(values, halos):
        return jnp.concatenate(
            [halos.reshape(2, HALO), values.reshape(2, run)], axis=1
        ).reshape(1, -1)

    def without_halos(values):
        return values.reshape(2, HALO + run)[:, HALO:].reshape(group_frames)

    stats = jnp.concatenate([with_halos(top, halo_top), with_halos(total, halo_total)], axis=0)
    gathered = lax.all_gather(stats, "frames", axis_index_groups=groups)
    all_top = lax.pmax(jnp.max(gathered[:, 0], axis=0), "centers")
    all_total = lax.psum(
        jnp.sum(gathered[:, 1] * jnp.exp2(ALPHA * (gathered[:, 0] - all_top)), axis=0),
        "centers",
    )

    device_frames = frames.shape[0]
    first = jnp.stack([device_at(outer, row, 0), device_at(outer, row, 4)]) * device_frames
    positions = first[:, None] + jnp.arange(-HALO, run, dtype=jnp.int32)[None, :]
    positions = positions.reshape(-1)
    usable = jnp.logical_and(
        segment_of(positions, starts) == segment_of(positions + LAG, starts),
        jnp.logical_and(positions >= 0, positions + LAG < device_frames * devices),
    )
    lead_tops = with_halos(lead_top, halo_lead_top)[0]
    lead_factor = jnp.where(usable, jnp.exp2(ALPHA * (lead_tops - all_top)) / all_total, 0.0)
    lag_factor = jnp.exp2(ALPHA * (with_halos(top, halo_top)[0] - all_top)) / all_total
    moved = lead_factor.reshape(2, HALO + run)[:, HALO - LAG : HALO - LAG + run]
    scale = moved.reshape(group_frames) * without_halos(lag_factor)
    return counts_of(lead, scale[None, :], member, outers)


def solution(mesh):
    return jax.shard_map(
        shards,
        mesh=mesh,
        in_specs=(P("frames", None), P("centers", None), P()),
        out_specs=P("frames", "centers"),
        check_vma=False,
    )
```

time: 145 us -> 131 us (0.903)
  Pallas kernels: 127 us -> 107 us
  blocking collectives: 9.57 us -> 13.2 us
  other arithmetic: 2.99 us -> 4.84 us
    pallas_call x2, Pallas kernels: 127 us -> 107 us  [the longest x1 54.1 us: members(): pl.pallas_call(members_kernel, in_specs=[anywhere, anywhere, anywhere], o...]
    all_gather x1, blocking collectives: 9.57 us -> 13.2 us  [shards(): gathered = lax.all_gather(stats, 'frames', axis_index_groups=groups)]
    pallas_call x0 -> x3, other arithmetic: none -> 1.75 us  [members(): pl.pallas_call(members_kernel, in_specs=[anywhere, anywhere, anywhere], o...]
    unnamed x9 -> x12, local copies, waits for them, and re-layouts: 2.28 us -> 3 us
where the time goes in v3:
time: 131 us
  Pallas kernels  107 us (82%)
  blocking collectives  13.2 us (10%)
  local copies, waits for them, and re-layouts  5.1 us (4%)
  other arithmetic  4.84 us (4%)
    pallas_call x1, Pallas kernels, members(): pl.pallas_call(members_kernel, in_specs=[anywhere, anywhere, anywhere], o...  54.1 us
    pallas_call x1, Pallas kernels, counts_of(): pl.pallas_call(functools.partial(counts_kernel, outers, K * K / (2 * fram...  53.1 us
    all_gather x1, blocking collectives, shards(): gathered = lax.all_gather(stats, 'frames', axis_index_groups=groups)  13.2 us
    unnamed x12, local copies, waits for them, and re-layouts  3 us

profile of v3, /device:TPU:0, one launch (start us, length us, event | category | flops | bytes accessed | tf_op | source)
XLA Modules:
  0.0 130.6 jit_solution(3895550942109168149)
XLA Ops:
  0.0 1.1 slice.16
  1.1 0.8 copy.8
  1.9 54.1 %members.1 = (bf16[2048,8192]{1,0:T(8,128)(2,1)}, bf16[512,8448]{1,0:T(8,128)(2,1)}, f32[16,1,512]{2,1,0:T(1,128)}, f32[16,1,512]{2,1,0:T(1,128)}, f32[16,1,512]...) custom-call(bf16[1024,512]{1,0:T(8,128)(2,1)} %frames_ref.1, ...), custom_call_target="tpu_custom_call" | custom-call | flops 21474836480 | bytes 50331648 | tf_op jit(solution)/shard_map/members/pallas_call | solution.py:279
  56.0 0.0 copy-start
  56.0 0.0 copy-start.3
  56.0 0.0 copy-start.1
  56.0 0.0 copy-start.2
  56.0 0.8 reduce.3
  56.9 0.7 maximum_bitcast_fusion.1
  57.6 0.8 reduce.2
  58.5 0.7 fusion.5
  59.3 0.1 maximum_bitcast_fusion
  59.3 13.2 %all-gather.1 = f32[8,2,8448]{2,1,0:T(2,128)S(1)} all-gather(f32[1,2,8448]{2,1,0:T(2,128)S(1)} %maximum_bitcast_fusion), channel_id=2, replica_groups={{0,1,2,3,8,9,10,11},{4,5,6,7,12,13,14,15},{16,17,18,19,24,25,26,27},{20..., dimensions={0}, use_global_device_ids=true | all-gather | bytes 608256 | tf_op jit(solution)/shard_map/all_gather | solution.py:555
  72.6 0.5 slice_reduce_fusion
  73.1 0.1 fusion.1
  73.3 0.0 copy-done
  73.3 0.1 reduce.1
  73.4 0.1 add_multiply_fusion
  73.5 0.1 broadcast_add_fusion.1
  73.7 0.6 convert_reduce_fusion
  74.3 0.2 fusion.12
  74.6 0.6 copy.14
  75.2 53.1 %counts.1 = f32[16,16384]{1,0:T(8,128)} custom-call(bf16[512,8448]{1,0:T(8,128)(2,1)} %get-tuple-element.13.lead_ref, f32[1,8192]{1,0:T(1,128)} %bitcast.41, bf16[2048,8192]{1,0:T(8,128)(2,1)} %get-tuple-element.20.member_ref), custom_call_target="tpu_custom_call" | custom-call | flops 17179869184 | bytes 41943040 | tf_op jit(solution)/shard_map/counts/pallas_call | solution.py:481
  128.4 2.3 %copy.22 = f32[16,16384]{1,0:T(8,128)} copy(f32[16,16384]{1,0:T(8,128)} %counts.1) | data formatting | bytes 2097152
  (15 shorter events, 0.3 us)
Async XLA Ops:
  56.0 17.3 %copy-start = (f32[16,1,512]{2,1,0:T(1,128)S(1)}, f32[16,1,512]{2,1,0:T(1,128)}, u32[]{:S(2)}) copy-start(f32[16,1,512]{2,1,0:T(1,128)} %get-tuple-element.15) | copy-start | bytes 98308
  56.0 17.6 %copy-start.3 = (s32[64]{0:T(128)S(1)}, s32[64]{0:T(128)}, u32[]{:S(2)}) copy-start(s32[64]{0:T(128)} %param.5) | copy-start | bytes 772
  56.0 18.3 %copy-start.1 = (f32[1,256]{1,0:T(1,128)S(1)}, f32[1,256]{1,0:T(1,128)}, u32[]{:S(2)}) copy-start(f32[1,256]{1,0:T(1,128)} %get-tuple-element.16) | copy-start | bytes 3076
  56.0 18.3 %copy-start.2 = (f32[1,256]{1,0:T(1,128)S(1)}, f32[1,256]{1,0:T(1,128)}, u32[]{:S(2)}) copy-start(f32[1,256]{1,0:T(1,128)} %get-tuple-element.14) | copy-start | bytes 3076

commit v4 on v3

--- a/solution.py
+++ b/solution.py
@@ -445,11 +445,11 @@
 
     def work(step, carry):
         pl.when(step < tiles)(lambda: compute(step))
-        pl.when(jnp.logical_and(step >= 2, step < tiles + 2))(lambda: merge(step - 2))
-        pl.when(step >= 5)(lambda: finish(step - 5))
+        pl.when(jnp.logical_and(step >= 1, step < tiles + 1))(lambda: merge(step - 1))
+        pl.when(step >= 4)(lambda: finish(step - 4))
         return carry
 
-    lax.fori_loop(0, tiles + 5, work, 0)
+    lax.fori_loop(0, tiles + 4, work, 0)
 
     def close(j, carry):
         for copy in halves(j):

time: 131 us -> 131 us (level)
  no operation moved by 1% of the time
where the time goes in v4:
time: 131 us
  Pallas kernels  107 us (82%)
  blocking collectives  13.2 us (10%)
  local copies, waits for them, and re-layouts  5.1 us (4%)
  other arithmetic  4.84 us (4%)
    pallas_call x1, Pallas kernels, members(): pl.pallas_call(members_kernel, in_specs=[anywhere, anywhere, anywhere], o...  54.1 us
    pallas_call x1, Pallas kernels, counts_of(): pl.pallas_call(functools.partial(counts_kernel, outers, K * K / (2 * fram...  53.4 us
    all_gather x1, blocking collectives, shards(): gathered = lax.all_gather(stats, 'frames', axis_index_groups=groups)  13.2 us
    unnamed x12, local copies, waits for them, and re-layouts  3 us

profile of v4, /device:TPU:0, one launch (start us, length us, event | category | flops | bytes accessed | tf_op | source)
XLA Modules:
  0.0 130.9 jit_solution(10588609982894939294)
XLA Ops:
  0.0 1.1 slice.16
  1.1 0.8 copy.8
  1.9 54.1 %members.1 = (bf16[2048,8192]{1,0:T(8,128)(2,1)}, bf16[512,8448]{1,0:T(8,128)(2,1)}, f32[16,1,512]{2,1,0:T(1,128)}, f32[16,1,512]{2,1,0:T(1,128)}, f32[16,1,512]...) custom-call(bf16[1024,512]{1,0:T(8,128)(2,1)} %frames_ref.1, ...), custom_call_target="tpu_custom_call" | custom-call | flops 21474836480 | bytes 50331648 | tf_op jit(solution)/shard_map/members/pallas_call | solution.py:279
  56.0 0.0 copy-start
  56.0 0.0 copy-start.3
  56.0 0.0 copy-start.1
  56.0 0.0 copy-start.2
  56.0 0.8 reduce.3
  56.9 0.7 maximum_bitcast_fusion.1
  57.6 0.8 reduce.2
  58.5 0.7 fusion.5
  59.3 0.1 maximum_bitcast_fusion
  59.3 13.2 %all-gather.1 = f32[8,2,8448]{2,1,0:T(2,128)S(1)} all-gather(f32[1,2,8448]{2,1,0:T(2,128)S(1)} %maximum_bitcast_fusion), channel_id=2, replica_groups={{0,1,2,3,8,9,10,11},{4,5,6,7,12,13,14,15},{16,17,18,19,24,25,26,27},{20..., dimensions={0}, use_global_device_ids=true | all-gather | bytes 608256 | tf_op jit(solution)/shard_map/all_gather | solution.py:555
  72.6 0.5 slice_reduce_fusion
  73.1 0.1 fusion.1
  73.3 0.0 copy-done
  73.3 0.1 reduce.1
  73.4 0.1 add_multiply_fusion
  73.5 0.1 broadcast_add_fusion.1
  73.7 0.6 convert_reduce_fusion
  74.3 0.2 fusion.12
  74.6 0.6 copy.14
  75.2 53.4 %counts.1 = f32[16,16384]{1,0:T(8,128)} custom-call(bf16[512,8448]{1,0:T(8,128)(2,1)} %get-tuple-element.13.lead_ref, f32[1,8192]{1,0:T(1,128)} %bitcast.41, bf16[2048,8192]{1,0:T(8,128)(2,1)} %get-tuple-element.20.member_ref), custom_call_target="tpu_custom_call" | custom-call | flops 17179869184 | bytes 41943040 | tf_op jit(solution)/shard_map/counts/pallas_call | solution.py:481
  128.6 2.3 %copy.22 = f32[16,16384]{1,0:T(8,128)} copy(f32[16,16384]{1,0:T(8,128)} %counts.1) | data formatting | bytes 2097152
  (15 shorter events, 0.3 us)
Async XLA Ops:
  56.0 17.3 %copy-start = (f32[16,1,512]{2,1,0:T(1,128)S(1)}, f32[16,1,512]{2,1,0:T(1,128)}, u32[]{:S(2)}) copy-start(f32[16,1,512]{2,1,0:T(1,128)} %get-tuple-element.15) | copy-start | bytes 98308
  56.0 17.6 %copy-start.3 = (s32[64]{0:T(128)S(1)}, s32[64]{0:T(128)}, u32[]{:S(2)}) copy-start(s32[64]{0:T(128)} %param.5) | copy-start | bytes 772
  56.0 18.3 %copy-start.1 = (f32[1,256]{1,0:T(1,128)S(1)}, f32[1,256]{1,0:T(1,128)}, u32[]{:S(2)}) copy-start(f32[1,256]{1,0:T(1,128)} %get-tuple-element.16) | copy-start | bytes 3076
  56.0 18.3 %copy-start.2 = (f32[1,256]{1,0:T(1,128)S(1)}, f32[1,256]{1,0:T(1,128)}, u32[]{:S(2)}) copy-start(f32[1,256]{1,0:T(1,128)} %get-tuple-element.14) | copy-start | bytes 3076
